TPU v7x, 256 devices: a whole 4x4x8 slice. The times are simulated.
256 devices in a mesh: tm: 8 (over z_hi, y), node: 32 (over x, z_lo, core).
Axes of the slice: x: 4, y: 4, z: 8 (z_hi: 2, z_lo: 4; z = z_hi * 4 + z_lo), core: 2. Of those that a mesh axis runs over, the one named last changes fastest.
Arguments:
- thermal_loading: bfloat16 [64, 4096], P(None, 'tm'), may hold values from -12 to 12
- forcing_matrix: bfloat16 [2048, 64], P('node'), may hold values from -0.75 to 0.75
- lagged_responses: float32 [2048, 256], P('node'), may hold values from 0 to 3, as said below
- pattern_heat_matrix: bfloat16 [2048, 32768], P(None, 'node'), may hold values from -0.03125 to 0.03125
- pattern_loading_matrix: bfloat16 [2048, 32768], P(None, 'node'), may hold values from -0.09375 to 0.09375
- starting_scale_depth: float32 [32768], P('node'), may hold values from 0.05 to 0.3
- point_parabolic_speed: float32 [32768], P('node'), may hold values from 1 to 3
Outputs:
- bond_heat_excursion: float32 [4096, 32768], P('tm', 'node')
- bond_loading: float32 [4096, 32768], P('tm', 'node')
- grown_layer_depth: float32 [4096, 32768], P('tm', 'node')
- fatigue_harm: float32 [4096, 32768], P('tm', 'node')
Inputs may be any that keep to these rules, and one draw needn't show every extreme that they name: `lagged_responses`: positive impulse responses.
All inputs are finite; a program needn't handle non-finite values.
Results may differ from a plain program's by a relative error of at most 0.0041.
Values may be sent and summed in bfloat16 or wider, within the bound.
A program may use at most 128 MiB of HBM per device.

v0:
```python
import functools

import jax
import jax.numpy as jnp
from jax import lax
from jax.experimental import pallas as pl
from jax.experimental.pallas import tpu as pltpu
from jax.sharding import PartitionSpec as P

MESH = pl.DeviceIdType.MESH
F32, BF16 = jnp.float32, jnp.bfloat16
RING = 4
CORES = 2
HALF = 256
COLS = 256
NT = (((1,), (1,)), ((), ()))


def dot(a, b):
    return jnp.dot(a, b, preferred_element_type=F32)


def split_dot(tri, values):
    high = values.astype(BF16)
    low = (values - high.astype(F32)).astype(BF16)
    return dot(tri, high) + dot(tri, low)


def kernel(
    tms, line,
    x_in, f_in, r_in, hh_in, hl_in, s0_in, p_in,
    heat, load, depth, harm,
    x2, fv, rv, r2, hh, hl, s0, p, halo, ys, yh, part, g, lhs, tri, tot, mine, rec,
    in_sem, halo_sem, ssem, rsem, xs, xr,
):
    tm = lax.axis_index("tm")
    me = lax.axis_index("node")
    core = lax.rem(me, CORES)
    z = lax.rem(me // CORES, line)
    x = me // (CORES * line)
    modes = f_in.shape[0]
    points = heat.shape[1]
    tiles = points // COLS

    def node(x, z, c):
        return (x * line + z) * CORES + c

    right, left, across = lax.rem(x + 1, RING), lax.rem(x + 3, RING), lax.rem(x + 2, RING)
    sib = node(x, z, 1 - core)
    to_right, to_left = node(right, z, core), node(left, z, core)
    if line == 4:
        upper = z // 2
        others = (1 - z + 4 * upper, 2 - upper, 3 - 3 * upper)
    else:
        others = (1 - z,)
    column = (z, *others)

    loads = [
        pltpu.make_async_copy(a, b, in_sem.at[i])
        for i, (a, b) in enumerate((
            (f_in, fv),
            (x_in, x2.at[pl.ds(modes, modes), :]),
            (x_in.at[:, pl.ds(0, HALF)], x2.at[pl.ds(0, modes), pl.ds(HALF, HALF)]),
            (r_in, rv.at[pl.ds(0, modes), :]),
            (r_in, rv.at[pl.ds(modes, modes), :]),
            (s0_in, s0),
            (p_in, p),
            (hh_in, hh),
            (hl_in, hl),
        ))
    ]
    for copy in loads:
        copy.start()

    barrier = pltpu.get_barrier_semaphore()
    for other in (sib, to_right, to_left, *(node(x, o, core) for o in others)):
        pl.semaphore_signal(barrier, inc=1, device_id=(tm, other), device_id_type=MESH)
    for d in range(1, tms):
        pl.semaphore_signal(barrier, inc=1, device_id=(lax.rem(tm + d, tms), me), device_id_type=MESH)

    x2[pl.ds(0, modes), pl.ds(0, HALF)] = jnp.zeros((modes, HALF), BF16)
    tri[...] = (
        lax.broadcasted_iota(jnp.int32, (HALF, HALF), 0)
        >= lax.broadcasted_iota(jnp.int32, (HALF, HALF), 1)
    ).astype(F32).astype(BF16)
    for copy in loads[:5]:
        copy.wait()

    both = 2 * modes
    twice = (
        lax.rem(lax.broadcasted_iota(jnp.int32, (both, modes), 0), modes)
        == lax.broadcasted_iota(jnp.int32, (both, modes), 1)
    ).astype(F32).astype(BF16)
    wide = lax.dot_general(dot(twice, fv[...]).astype(BF16), twice, NT, preferred_element_type=F32)
    same = (
        lax.broadcasted_iota(jnp.int32, (both, both), 0) // modes
        == lax.broadcasted_iota(jnp.int32, (both, both), 1) // modes
    )
    drive = jnp.where(same, wide, 0.0).astype(BF16)

    def driven(source):
        return lax.dot_general(
            source.astype(F32).T.astype(BF16), drive, NT, preferred_element_type=F32
        )

    r2[...] = rv[...].T
    y = driven(x2[...])
    for s in range(8):
        ys[s] = y if s == 0 else pltpu.roll(y, s, 0)

    def lags(source, rows):
        def some(a, total):
            at = pl.multiple_of(HALF - 8 * a, 8)
            weights = r2[pl.ds(pl.multiple_of(8 * a, 8), 8), :]
            for s in range(8):
                total = total + weights[s : s + 1, :] * source[s, pl.ds(at, rows), :]
            return total

        return some

    local = lax.fori_loop(0, HALF // 8, lags(ys, HALF), jnp.zeros((HALF, both), F32)).T
    part[...] = local[:modes]
    g[0, me] = local[modes:].astype(BF16)

    pl.semaphore_wait(barrier, 3 + len(others) + tms - 1)

    def halo_copy():
        return pltpu.make_async_remote_copy(
            src_ref=x2.at[pl.ds(modes, modes), pl.ds(HALF, HALF)],
            dst_ref=halo,
            send_sem=halo_sem.at[0],
            recv_sem=halo_sem.at[1],
            device_id=(lax.rem(tm + 1, tms), me),
            device_id_type=MESH,
        )

    def block(q, of, to, i):
        return pltpu.make_async_remote_copy(
            src_ref=g.at[q, of],
            dst_ref=g.at[q, of],
            send_sem=ssem.at[q, i],
            recv_sem=rsem.at[q, of],
            device_id=(tm, to),
            device_id_type=MESH,
        )

    def arrived(q, of):
        block(q, of, sib, 0).wait_recv()

    sent = [0, 0]

    def send(q, of, to):
        block(q, of, to, sent[q]).start()
        sent[q] += 1

    def own(q):
        send(q, me, to_right)
        send(q, me, to_left)
        for o in others:
            send(q, me, node(x, o, core))
        send(q, me, sib)

    def along_line(q):
        for o in others:
            of = node(x, o, core)
            arrived(q, of)
            send(q, of, to_right)
            send(q, of, to_left)
            send(q, of, sib)

    def along_ring(q, o):
        a, b = node(left, o, core), node(right, o, core)
        even = 1 - lax.rem(o, 2)
        first = even * a + (1 - even) * b
        second = (1 - even) * a + even * b
        arrived(q, first)
        send(q, first, even * to_right + (1 - even) * to_left)
        send(q, first, sib)
        arrived(q, second)
        send(q, second, sib)

    def far_side(q, o):
        of = node(across, o, core)
        arrived(q, of)
        send(q, of, sib)

    def turn(q):
        for xs_ in (x, left, right, across):
            for o in column:
                chip = xs_ * line + o
                arrived(q, chip * CORES + 1 - core)
                both_cores = g[q, pl.ds(chip * CORES, CORES)].reshape(both, HALF)
                lhs[q, :, pl.ds(pl.multiple_of(chip * both, both), both)] = both_cores.T

    def rows(q):
        return pl.ds(HALF * (1 - q), HALF)

    def tile(j):
        return pl.ds(pl.multiple_of(j * COLS, COLS), COLS)

    def heat_tile(q, j):
        cols = tile(j)
        value = dot(lhs[q], hh[:, cols])
        heat[rows(q), cols] = value
        within = split_dot(tri[...], p[:, cols] * jnp.exp(0.5 * value))
        depth[rows(q), cols] = within
        tot[q, :, cols] = within[HALF - 1 :, :]

    def load_tile(q, j):
        cols = tile(j)
        load[rows(q), cols] = dot(lhs[q], hl[:, cols])

    @pl.when(tm + 1 < tms)
    def _():
        halo_copy().start()

    own(0)
    along_line(0)

    @pl.when(tm > 0)
    def _():
        halo_copy().wait_recv()

    @pl.when(tm == 0)
    def _():
        halo[...] = jnp.zeros_like(halo)

    before = halo[...]
    shifted = jnp.concatenate([before[:, both:], jnp.zeros((modes, HALF - both), BF16)], axis=1)
    y = driven(jnp.concatenate([before, shifted], axis=0))
    y = jnp.concatenate([y, jnp.zeros((64, both), F32)], axis=0)
    for s in range(8):
        yh[s] = y if s == 0 else pltpu.roll(y, s, 0)
    first = lax.fori_loop(0, 8, lags(yh, 64), jnp.zeros((64, both), F32))
    first = jnp.concatenate([first, jnp.zeros((both - 64, both), F32)], axis=0)
    late = lax.fori_loop(8, HALF // 8, lags(yh, both), first).T
    late = jnp.concatenate([late[:modes], late[modes:]], axis=1)
    g[1, me] = (part[...] + late).astype(BF16)

    own(1)
    for o in column:
        along_ring(0, o)
    along_line(1)
    for o in column:
        far_side(0, o)
    turn(0)
    for copy in loads[5:]:
        copy.wait()
    for j, o in enumerate(column):
        if j < tiles:
            heat_tile(0, j)
        along_ring(1, o)
    for j, o in enumerate(column):
        if j < tiles:
            load_tile(0, j)
        far_side(1, o)
    turn(1)

    def over(count, one):
        lax.fori_loop(0, count, lambda j, _: (one(j), None)[1], None)

    over(tiles, functools.partial(heat_tile, 1))

    def total_copy(stage, d):
        return pltpu.make_async_remote_copy(
            src_ref=mine.at[stage],
            dst_ref=rec.at[stage, tm],
            send_sem=xs.at[stage, d],
            recv_sem=xr.at[stage, tm],
            device_id=(lax.rem(tm + d, tms), me),
            device_id_type=MESH,
        )

    def give(stage):
        mine[stage] = tot[2 * stage] + tot[2 * stage + 1]
        for d in range(tms - 1, 0, -1):

            @pl.when(tm + d < tms)
            def _():
                total_copy(stage, d).start()

    def take(stage):
        def one(i, total):
            pltpu.make_async_remote_copy(
                src_ref=mine.at[stage],
                dst_ref=rec.at[stage, i],
                send_sem=xs.at[stage, 0],
                recv_sem=xr.at[stage, i],
                device_id=(lax.rem(tm + 1, tms), me),
                device_id_type=MESH,
            ).wait_recv()
            return total + rec[stage, i]

        return lax.fori_loop(0, tm, one, jnp.zeros((1, points), F32))

    give(0)
    over(tiles, functools.partial(load_tile, 1))
    share = 8.0 / (2 * HALF * tms)
    earlier = take(0)
    rec[0, tm] = s0[...] * s0[...] + share * earlier

    def depth_tile(q, j):
        cols = tile(j)
        base = rec[0, tm, :, cols]
        if q == 0:
            base = base + share * tot[1, :, cols]
        square = base + share * depth[rows(q), cols]
        layer = square * lax.rsqrt(square)
        depth[rows(q), cols] = layer
        stress = load[rows(q), cols] * (5.0 - 40.0 / (layer + 10.0))
        within = split_dot(tri[...], stress * stress)
        harm[rows(q), cols] = within
        tot[2 + q, :, cols] = within[HALF - 1 :, :]

    over(tiles, functools.partial(depth_tile, 1))
    over(tiles, functools.partial(depth_tile, 0))
    give(1)
    rec[1, tm] = take(1)

    def harm_tile(q, j):
        cols = tile(j)
        base = rec[1, tm, :, cols]
        if q == 0:
            base = base + tot[3, :, cols]
        harm[rows(q), cols] = (harm[rows(q), cols] + base) * (1.0 / (2 * HALF * tms))

    over(tiles, functools.partial(harm_tile, 1))
    over(tiles, functools.partial(harm_tile, 0))

    @pl.when(tm + 1 < tms)
    def _():
        halo_copy().wait_send()

    for stage in range(2):
        for d in range(1, tms):

            @pl.when(tm + d < tms)
            def _():
                total_copy(stage, d).wait_send()

    for q in range(2):
        for i in range(sent[q]):
            block(q, me, sib, i).wait_send()


def shards(tms, line, x, f, r, hh, hl, s0, p):
    modes, lags = r.shape
    steps = x.shape[1]
    points = hh.shape[1]
    nodes = RING * line * CORES
    every = nodes * modes
    hbm = pl.BlockSpec(memory_space=pltpu.HBM)
    vmem = pl.BlockSpec(memory_space=pltpu.VMEM)
    dma = pltpu.SemaphoreType.DMA
    sends = 2 + line - 1 + 1 + 3 * (line - 1) + 3 * line + line
    arrays = (x, f, r, hh, hl, s0.reshape(1, points), p.reshape(1, points))
    return pl.pallas_call(
        functools.partial(kernel, tms, line),
        out_shape=[pltpu.VMEM((steps, points), F32)] * 4,
        in_specs=[hbm] * 7,
        out_specs=[vmem] * 4,
        scratch_shapes=[
            pltpu.VMEM((2 * modes, steps), BF16),
            pltpu.VMEM(f.shape, BF16),
            pltpu.VMEM((2 * modes, lags), F32),
            pltpu.VMEM((lags, 2 * modes), F32),
            pltpu.VMEM(hh.shape, BF16),
            pltpu.VMEM(hl.shape, BF16),
            pltpu.VMEM((1, points), F32),
            pltpu.VMEM((1, points), F32),
            pltpu.VMEM((modes, HALF), BF16),
            pltpu.VMEM((8, steps, 2 * modes), F32),
            pltpu.VMEM((8, HALF + 64, 2 * modes), F32),
            pltpu.VMEM((modes, HALF), F32),
            pltpu.VMEM((2, nodes, modes, HALF), BF16),
            pltpu.VMEM((2, HALF, every), BF16),
            pltpu.VMEM((HALF, HALF), BF16),
            pltpu.VMEM((4, 1, points), F32),
            pltpu.VMEM((2, 1, points), F32),
            pltpu.VMEM((2, tms, 1, points), F32),
            dma((9,)),
            dma((2,)),
            dma((2, sends)),
            dma((2, nodes)),
            dma((2, tms)),
            dma((2, tms)),
        ],
        compiler_params=pltpu.CompilerParams(
            collective_id=0, has_side_effects=True, vmem_limit_bytes=40 * 1024 * 1024
        ),
    )(*(pltpu.with_memory_space_constraint(a, pltpu.HBM) for a in arrays))


def solution(mesh):
    tms, nodes = mesh.shape["tm"], mesh.shape["node"]
    return jax.shard_map(
        functools.partial(shards, tms, nodes // (RING * CORES)),
        mesh=mesh,
        in_specs=(
            P(None, "tm"),
            P("node", None),
            P("node", None),
            P(None, "node"),
            P(None, "node"),
            P("node"),
            P("node"),
        ),
        out_specs=(P("tm", "node"),) * 4,
        check_vma=False,
    )
```

profile of v0, /device:TPU:224, one launch (start us, length us, event | category | flops | bytes accessed | tf_op | source)
XLA Modules:
  0.0 50.9 jit_solution(11651137678917595301)
XLA Ops:
  0.6 45.0 %shard_map.102 = (f32[512,1024]{1,0:T(8,128)S(1)}, f32[512,1024]{1,0:T(8,128)S(1)}, f32[512,1024]{1,0:T(8,128)S(1)}, f32[512,1024]{1,0:T(8,128)S(1)}) custom-call(bf16[64,512]{1,0:T(8,128)(2,1)} %x_in.1, bf16[64,64]{1,0:T(8,128)(2,1)} %f_in.1, f32[64,256]{1,0:T(8,128)} %r_in.1, bf16[2048,1024]{1,0:T(8,128)(2,1)} %hh_in.1, bf16[2048,1024]{1,0:T(8,128)(2,1)} %hl_in.1, ...), custom_call_target="tpu_custom_call" | custom-call | tf_op jit(solution)/shard_map/pallas_call | solution.py:357
  45.6 1.3 %copy.15 = f32[512,1024]{1,0:T(8,128)} copy(f32[512,1024]{1,0:T(8,128)S(1)} %get-tuple-element.4) | data formatting | bytes 4194304
  47.0 1.3 %copy.16 = f32[512,1024]{1,0:T(8,128)} copy(f32[512,1024]{1,0:T(8,128)S(1)} %get-tuple-element.5) | data formatting | bytes 4194304
  48.3 1.3 %copy.17 = f32[512,1024]{1,0:T(8,128)} copy(f32[512,1024]{1,0:T(8,128)S(1)} %get-tuple-element.6) | data formatting | bytes 4194304
  49.6 1.3 %copy.18 = f32[512,1024]{1,0:T(8,128)} copy(f32[512,1024]{1,0:T(8,128)S(1)} %get-tuple-element.7) | data formatting | bytes 4194304
where the time goes:
time: 51.7 us; the launch traced here: 50.9 us
  Pallas kernels  45 us (87%)
  local copies, waits for them, and re-layouts  5.28 us (10%)
  between operations  0.64 us (1%)
    pallas_call x1, Pallas kernels, shards(): pl.pallas_call(functools.partial(kernel, tms, line), out_shape=[pltpu.VME...  45 us
    unnamed x4, local copies, waits for them, and re-layouts  5.28 us

commit v1 on v0

--- a/solution.py
+++ b/solution.py
@@ -13,6 +13,7 @@
 CORES = 2
 HALF = 256
 COLS = 256
+PIECES = 2
 NT = (((1,), (1,)), ((), ()))
 
 
@@ -31,7 +32,7 @@
     x_in, f_in, r_in, hh_in, hl_in, s0_in, p_in,
     heat, load, depth, harm,
     x2, fv, rv, r2, hh, hl, s0, p, halo, ys, yh, part, g, lhs, tri, tot, mine, rec,
-    in_sem, halo_sem, ssem, rsem, xs, xr,
+    in_sem, halo_sem, ssem, rsem, bsem, xs, xr,
 ):
     tm = lax.axis_index("tm")
     me = lax.axis_index("node")
@@ -47,13 +48,18 @@
 
     right, left, across = lax.rem(x + 1, RING), lax.rem(x + 3, RING), lax.rem(x + 2, RING)
     sib = node(x, z, 1 - core)
-    to_right, to_left = node(right, z, core), node(left, z, core)
+    others_x = (right, left, across)
+    along_x = tuple(node(o, z, core) for o in others_x)
     if line == 4:
         upper = z // 2
         others = (1 - z + 4 * upper, 2 - upper, 3 - 3 * upper)
     else:
         others = (1 - z,)
-    column = (z, *others)
+    along_z = tuple(node(x, o, core) for o in others)
+    near = [(x, z), *((x, o) for o in others), *((o, z) for o in others_x)]
+    far = [(a, b) for b in others for a in others_x]
+    chips = [a * line + b for a, b in near + far]
+    both = CORES * modes
 
     loads = [
         pltpu.make_async_copy(a, b, in_sem.at[i])
@@ -65,19 +71,29 @@
             (r_in, rv.at[pl.ds(modes, modes), :]),
             (s0_in, s0),
             (p_in, p),
-            (hh_in, hh),
-            (hl_in, hl),
         ))
     ]
+
+    def pattern_loads(i):
+        there = pl.ds(pl.multiple_of(chips[i] * both, both), both)
+        here = pl.ds(i * both, both)
+        return [
+            pltpu.make_async_copy(a.at[there], b.at[here], in_sem.at[7 + 2 * i + k])
+            for k, (a, b) in enumerate(((hh_in, hh), (hl_in, hl)))
+        ]
+
     for copy in loads:
         copy.start()
 
     barrier = pltpu.get_barrier_semaphore()
-    for other in (sib, to_right, to_left, *(node(x, o, core) for o in others)):
+    for other in (sib, *along_x, *along_z):
         pl.semaphore_signal(barrier, inc=1, device_id=(tm, other), device_id_type=MESH)
     for d in range(1, tms):
         pl.semaphore_signal(barrier, inc=1, device_id=(lax.rem(tm + d, tms), me), device_id_type=MESH)
 
+    for i in range(len(chips)):
+        for copy in pattern_loads(i):
+            copy.start()
     x2[pl.ds(0, modes), pl.ds(0, HALF)] = jnp.zeros((modes, HALF), BF16)
     tri[...] = (
         lax.broadcasted_iota(jnp.int32, (HALF, HALF), 0)
@@ -86,7 +102,6 @@
     for copy in loads[:5]:
         copy.wait()
 
-    both = 2 * modes
     twice = (
         lax.rem(lax.broadcasted_iota(jnp.int32, (both, modes), 0), modes)
         == lax.broadcasted_iota(jnp.int32, (both, modes), 1)
@@ -122,7 +137,7 @@
     part[...] = local[:modes]
     g[0, me] = local[modes:].astype(BF16)
 
-    pl.semaphore_wait(barrier, 3 + len(others) + tms - 1)
+    pl.semaphore_wait(barrier, 4 + len(others) + tms - 1)
 
     def halo_copy():
         return pltpu.make_async_remote_copy(
@@ -134,88 +149,90 @@
             device_id_type=MESH,
         )
 
-    def block(q, of, to, i):
+    cut = modes * 3 // 4
+    whole, by_line, by_ring = (0, modes), (0, cut), (cut, modes - cut)
+
+    def block(q, of, to, i, part):
+        place = g.at[q, of, pl.ds(*part)]
         return pltpu.make_async_remote_copy(
-            src_ref=g.at[q, of],
-            dst_ref=g.at[q, of],
+            src_ref=place,
+            dst_ref=place,
             send_sem=ssem.at[q, i],
-            recv_sem=rsem.at[q, of],
+            recv_sem=(bsem if part == by_ring else rsem).at[q, of],
             device_id=(tm, to),
             device_id_type=MESH,
         )
 
-    def arrived(q, of):
-        block(q, of, sib, 0).wait_recv()
-
-    sent = [0, 0]
-
-    def send(q, of, to):
-        block(q, of, to, sent[q]).start()
-        sent[q] += 1
+    def arrived(q, of, part):
+        block(q, of, sib, 0, part).wait_recv()
+
+    sent = [[], []]
+
+    def send(q, of, to, part):
+        block(q, of, to, len(sent[q]), part).start()
+        sent[q].append(part)
 
     def own(q):
-        send(q, me, to_right)
-        send(q, me, to_left)
-        for o in others:
-            send(q, me, node(x, o, core))
-        send(q, me, sib)
-
-    def along_line(q):
-        for o in others:
-            of = node(x, o, core)
-            arrived(q, of)
-            send(q, of, to_right)
-            send(q, of, to_left)
-            send(q, of, sib)
-
-    def along_ring(q, o):
-        a, b = node(left, o, core), node(right, o, core)
-        even = 1 - lax.rem(o, 2)
-        first = even * a + (1 - even) * b
-        second = (1 - even) * a + even * b
-        arrived(q, first)
-        send(q, first, even * to_right + (1 - even) * to_left)
-        send(q, first, sib)
-        arrived(q, second)
-        send(q, second, sib)
-
-    def far_side(q, o):
-        of = node(across, o, core)
-        arrived(q, of)
-        send(q, of, sib)
-
-    def turn(q):
-        for xs_ in (x, left, right, across):
-            for o in column:
-                chip = xs_ * line + o
-                arrived(q, chip * CORES + 1 - core)
-                both_cores = g[q, pl.ds(chip * CORES, CORES)].reshape(both, HALF)
-                lhs[q, :, pl.ds(pl.multiple_of(chip * both, both), both)] = both_cores.T
+        order = (along_z[0], *along_x[:2], *along_z[1:], along_x[2], sib)
+        for to in order:
+            send(q, me, to, whole)
+
+    def line_in(q, i):
+        of = along_z[i]
+        arrived(q, of, whole)
+        for to in along_x:
+            send(q, of, to, by_line)
+        send(q, of, sib, whole)
+
+    def ring_in(q, i):
+        of = along_x[i]
+        arrived(q, of, whole)
+        for to in along_z:
+            send(q, of, to, by_ring)
+        send(q, of, sib, whole)
+
+    def far_in(q, i):
+        of = node(*far[i], core)
+        arrived(q, of, by_line)
+        arrived(q, of, by_ring)
+        send(q, of, sib, whole)
+
+    def turn(q, some):
+        for i in some:
+            arrived(q, chips[i] * CORES + 1 - core, whole)
+            both_cores = g[q, pl.ds(chips[i] * CORES, CORES)].reshape(both, HALF)
+            lhs[q, :, pl.ds(i * both, both)] = both_cores.T
 
     def rows(q):
         return pl.ds(HALF * (1 - q), HALF)
 
     def tile(j):
-        return pl.ds(pl.multiple_of(j * COLS, COLS), COLS)
-
-    def heat_tile(q, j):
-        cols = tile(j)
-        value = dot(lhs[q], hh[:, cols])
-        heat[rows(q), cols] = value
-        within = split_dot(tri[...], p[:, cols] * jnp.exp(0.5 * value))
-        depth[rows(q), cols] = within
-        tot[q, :, cols] = within[HALF - 1 :, :]
-
-    def load_tile(q, j):
-        cols = tile(j)
-        load[rows(q), cols] = dot(lhs[q], hl[:, cols])
+        return pl.ds(j * COLS, COLS)
+
+    group = len(chips) // 2
+    span = group * both
+
+    def add_group(out, patterns, q, k):
+        some = pl.ds(k * span, span)
+        value = dot(lhs[q, :, some], patterns[some, :])
+        out[rows(q), :] = value if k == 0 else out[rows(q), :] + value
+
+    def grow(q):
+        for j in range(tiles):
+            cols = tile(j)
+            growth = p[:, cols] * jnp.exp(0.5 * heat[rows(q), cols])
+            within = split_dot(tri[...], growth)
+            depth[rows(q), cols] = within
+            tot[q, :, cols] = within[HALF - 1 :, :]
 
     @pl.when(tm + 1 < tms)
     def _():
         halo_copy().start()
 
     own(0)
-    along_line(0)
+    line_in(0, 0)
+    ring_in(0, 0)
+    ring_in(0, 1)
 
     @pl.when(tm > 0)
     def _():
@@ -238,28 +255,48 @@
     g[1, me] = (part[...] + late).astype(BF16)
 
     own(1)
-    for o in column:
-        along_ring(0, o)
-    along_line(1)
-    for o in column:
-        far_side(0, o)
-    turn(0)
+    for i in range(1, len(others)):
+        line_in(0, i)
+    ring_in(0, 2)
+    n_near, n_far = len(near), len(far)
+    soon = 2 * n_far // 3
+    turn(0, range(n_near))
+    line_in(1, 0)
+    ring_in(1, 0)
+    ring_in(1, 1)
+    for i in range(n_far // 2):
+        far_in(0, i)
+    turn(0, range(n_near, group))
     for copy in loads[5:]:
         copy.wait()
-    for j, o in enumerate(column):
-        if j < tiles:
-            heat_tile(0, j)
-        along_ring(1, o)
-    for j, o in enumerate(column):
-        if j < tiles:
-            load_tile(0, j)
-        far_side(1, o)
-    turn(1)
+    for i in range(len(chips)):
+        for copy in pattern_loads(i):
+            copy.wait()
+    add_group(heat, hh, 0, 0)
+    for i in range(1, len(others)):
+        line_in(1, i)
+    ring_in(1, 2)
+    for i in range(n_far // 2, n_far):
+        far_in(0, i)
+    add_group(load, hl, 0, 0)
+    turn(0, range(max(n_near, group), n_near + n_far))
+    add_group(heat, hh, 0, 1)
+    for i in range(soon):
+        far_in(1, i)
+    turn(1, range(group))
+    add_group(load, hl, 0, 1)
+    grow(0)
+    add_group(heat, hh, 1, 0)
+    for i in range(soon, n_far):
+        far_in(1, i)
+    add_group(load, hl, 1, 0)
+    turn(1, range(group, n_near + n_far))
+    add_group(heat, hh, 1, 1)
+    grow(1)
 
     def over(count, one):
-        lax.fori_loop(0, count, lambda j, _: (one(j), None)[1], None)
-
-    over(tiles, functools.partial(heat_tile, 1))
+        for j in range(count):
+            one(j)
 
     def total_copy(stage, d):
         return pltpu.make_async_remote_copy(
@@ -294,7 +331,7 @@
         return lax.fori_loop(0, tm, one, jnp.zeros((1, points), F32))
 
     give(0)
-    over(tiles, functools.partial(load_tile, 1))
+    add_group(load, hl, 1, 1)
     share = 8.0 / (2 * HALF * tms)
     earlier = take(0)
     rec[0, tm] = s0[...] * s0[...] + share * earlier
@@ -339,8 +376,24 @@
                 total_copy(stage, d).wait_send()
 
     for q in range(2):
-        for i in range(sent[q]):
-            block(q, me, sib, i).wait_send()
+        for i, part_sent in enumerate(sent[q]):
+            block(q, me, sib, i, part_sent).wait_send()
+
+
+def writer(*refs):
+    sem = refs[8]
+    size = refs[0].shape[0] // PIECES
+    copies = [
+        pltpu.make_async_copy(
+            refs[i].at[pl.ds(k * size, size)], refs[4 + i].at[pl.ds(k * size, size)], sem.at[i, k]
+        )
+        for i in range(4)
+        for k in range(PIECES)
+    ]
+    for copy in copies:
+        copy.start()
+    for copy in copies:
+        copy.wait()
 
 
 def shards(tms, line, x, f, r, hh, hl, s0, p):
@@ -352,9 +405,9 @@
     hbm = pl.BlockSpec(memory_space=pltpu.HBM)
     vmem = pl.BlockSpec(memory_space=pltpu.VMEM)
     dma = pltpu.SemaphoreType.DMA
-    sends = 2 + line - 1 + 1 + 3 * (line - 1) + 3 * line + line
+    sends = (line + 3) + 4 * (line - 1) + 3 * line + 3 * (line - 1)
     arrays = (x, f, r, hh, hl, s0.reshape(1, points), p.reshape(1, points))
-    return pl.pallas_call(
+    results = pl.pallas_call(
         functools.partial(kernel, tms, line),
         out_shape=[pltpu.VMEM((steps, points), F32)] * 4,
         in_specs=[hbm] * 7,
@@ -378,9 +431,10 @@
             pltpu.VMEM((4, 1, points), F32),
             pltpu.VMEM((2, 1, points), F32),
             pltpu.VMEM((2, tms, 1, points), F32),
-            dma((9,)),
+            dma((7 + 2 * RING * line,)),
             dma((2,)),
             dma((2, sends)),
+            dma((2, nodes)),
             dma((2, nodes)),
             dma((2, tms)),
             dma((2, tms)),
@@ -389,6 +443,14 @@
             collective_id=0, has_side_effects=True, vmem_limit_bytes=40 * 1024 * 1024
         ),
     )(*(pltpu.with_memory_space_constraint(a, pltpu.HBM) for a in arrays))
+    return pl.pallas_call(
+        writer,
+        out_shape=[jax.ShapeDtypeStruct((steps, points), F32)] * 4,
+        in_specs=[vmem] * 4,
+        out_specs=[pl.BlockSpec(memory_space=pl.ANY)] * 4,
+        scratch_shapes=[dma((4, PIECES))],
+        compiler_params=pltpu.CompilerParams(vmem_limit_bytes=4 * 1024 * 1024),
+    )(*results)
 
 
 def solution(mesh):

time: 51.7 us -> 43.4 us (0.84); the launches traced: 50.9 us -> 43.3 us
  local copies, waits for them, and re-layouts: 5.28 us -> 0 us
  Pallas kernels: 45 us -> 42.6 us
    pallas_call x1, Pallas kernels: 45 us -> 39.2 us  [shards(): pl.pallas_call(functools.partial(kernel, tms, line), out_shape=[pltpu.VME...]
    unnamed x4 -> x0, local copies, waits for them, and re-layouts: 5.28 us -> none
    pallas_call x0 -> x1, Pallas kernels: none -> 3.37 us  [shards(): pl.pallas_call(writer, out_shape=[jax.ShapeDtypeStruct((steps, points), F...]
where the time goes in v1:
time: 43.4 us; the launch traced here: 43.3 us
  Pallas kernels  42.6 us (98%)
  between operations  0.64 us (1%)
    pallas_call x1, Pallas kernels, shards(): pl.pallas_call(functools.partial(kernel, tms, line), out_shape=[pltpu.VME...  39.2 us
    pallas_call x1, Pallas kernels, shards(): pl.pallas_call(writer, out_shape=[jax.ShapeDtypeStruct((steps, points), F...  3.37 us

profile of v1, /device:TPU:224, one launch (start us, length us, event | category | flops | bytes accessed | tf_op | source)
XLA Modules:
  0.0 43.3 jit_solution(17526191257194386330)
XLA Ops:
  0.6 39.2 %shard_map.102 = (f32[512,1024]{1,0:T(8,128)S(1)}, f32[512,1024]{1,0:T(8,128)S(1)}, f32[512,1024]{1,0:T(8,128)S(1)}, f32[512,1024]{1,0:T(8,128)S(1)}) custom-call(bf16[64,512]{1,0:T(8,128)(2,1)} %x_in.1, bf16[64,64]{1,0:T(8,128)(2,1)} %f_in.1, f32[64,256]{1,0:T(8,128)} %r_in.1, bf16[2048,1024]{1,0:T(8,128)(2,1)} %hh_in.1, bf16[2048,1024]{1,0:T(8,128)(2,1)} %hl_in.1, ...), custom_call_target="tpu_custom_call" | custom-call | tf_op jit(solution)/shard_map/pallas_call | solution.py:410
  39.9 3.4 %shard_map.103 = (f32[512,1024]{1,0:T(8,128)}, f32[512,1024]{1,0:T(8,128)}, f32[512,1024]{1,0:T(8,128)}, f32[512,1024]{1,0:T(8,128)}) custom-call(f32[512,1024]{1,0:T(8,128)S(1)} %get-tuple-element.8.refs_0_, f32[512,1024]{1,0:T(8,128)S(1)} %get-tuple-element.9.refs_1_, f32[512,1024]{1,0:T(8,128)S(1)} %get-tuple-element.10.refs_2_, ...), custom_call_target="tpu_custom_call" | custom-call | tf_op jit(solution)/shard_map/pallas_call | solution.py:446

commit v2 on v1

--- a/solution.py
+++ b/solution.py
@@ -31,8 +31,8 @@
     tms, line,
     x_in, f_in, r_in, hh_in, hl_in, s0_in, p_in,
     heat, load, depth, harm,
-    x2, fv, rv, r2, hh, hl, s0, p, halo, ys, yh, part, g, lhs, tri, tot, mine, rec,
-    in_sem, halo_sem, ssem, rsem, bsem, xs, xr,
+    x2, fv, rv, r2, hh, hl, s0, p, halo, ys, yh, g, lhs, tri, tot, mine, rec,
+    in_sem, halo_sem, ssem, rsem, bsem, xs, xr, ready,
 ):
     tm = lax.axis_index("tm")
     me = lax.axis_index("node")
@@ -56,9 +56,8 @@
     else:
         others = (1 - z,)
     along_z = tuple(node(x, o, core) for o in others)
-    near = [(x, z), *((x, o) for o in others), *((o, z) for o in others_x)]
-    far = [(a, b) for b in others for a in others_x]
-    chips = [a * line + b for a, b in near + far]
+    columns = (x, *others_x)
+    chips = [a * line + b for a in columns for b in range(line)]
     both = CORES * modes
 
     loads = [
@@ -89,7 +88,15 @@
     for other in (sib, *along_x, *along_z):
         pl.semaphore_signal(barrier, inc=1, device_id=(tm, other), device_id_type=MESH)
     for d in range(1, tms):
-        pl.semaphore_signal(barrier, inc=1, device_id=(lax.rem(tm + d, tms), me), device_id_type=MESH)
+
+        @pl.when(tm + d < tms)
+        def _():
+            pl.semaphore_signal(barrier, inc=1, device_id=(tm + d, me), device_id_type=MESH)
+
+    @pl.when(tm > 0)
+    def _():
+        pl.semaphore_signal(barrier, inc=1, device_id=(tm - 1, me), device_id_type=MESH)
+
 
     for i in range(len(chips)):
         for copy in pattern_loads(i):
@@ -133,11 +140,10 @@
 
         return some
 
-    local = lax.fori_loop(0, HALF // 8, lags(ys, HALF), jnp.zeros((HALF, both), F32)).T
-    part[...] = local[:modes]
-    g[0, me] = local[modes:].astype(BF16)
-
-    pl.semaphore_wait(barrier, 4 + len(others) + tms - 1)
+    groups = HALF // 8
+    local = lax.fori_loop(0, groups // 2, lags(ys, HALF), jnp.zeros((HALF, both), F32))
+
+    pl.semaphore_wait(barrier, 4 + len(others) + tm + 1 - (tm + 1) // tms)
 
     def halo_copy():
         return pltpu.make_async_remote_copy(
@@ -149,59 +155,70 @@
             device_id_type=MESH,
         )
 
-    cut = modes * 3 // 4
-    whole, by_line, by_ring = (0, modes), (0, cut), (cut, modes - cut)
-
-    def block(q, of, to, i, part):
-        place = g.at[q, of, pl.ds(*part)]
+    def block(q, a, b, to, i):
+        place = g.at[q, core, a, b]
         return pltpu.make_async_remote_copy(
             src_ref=place,
             dst_ref=place,
             send_sem=ssem.at[q, i],
-            recv_sem=(bsem if part == by_ring else rsem).at[q, of],
+            recv_sem=rsem.at[q, a * line + b],
             device_id=(tm, to),
             device_id_type=MESH,
         )
 
-    def arrived(q, of, part):
-        block(q, of, sib, 0, part).wait_recv()
-
-    sent = [[], []]
-
-    def send(q, of, to, part):
-        block(q, of, to, len(sent[q]), part).start()
-        sent[q].append(part)
+    def whole(q, a, c, i):
+        place = g.at[q, c, a]
+        return pltpu.make_async_remote_copy(
+            src_ref=place,
+            dst_ref=place,
+            send_sem=bsem.at[0, q, i],
+            recv_sem=bsem.at[1, q, a],
+            device_id=(tm, sib),
+            device_id_type=MESH,
+        )
+
+    def arrived(q, a, b):
+        block(q, a, b, sib, 0).wait_recv()
+
+    sent = [0, 0]
+
+    def send(q, a, b, to):
+        block(q, a, b, to, sent[q]).start()
+        sent[q] += 1
 
     def own(q):
-        order = (along_z[0], *along_x[:2], *along_z[1:], along_x[2], sib)
-        for to in order:
-            send(q, me, to, whole)
+        for to in (*along_z[1:], *along_x[:2], along_z[0], along_x[2]):
+            send(q, x, z, to)
 
     def line_in(q, i):
-        of = along_z[i]
-        arrived(q, of, whole)
-        for to in along_x:
-            send(q, of, to, by_line)
-        send(q, of, sib, whole)
+        arrived(q, x, others[i])
+        if i > 0:
+            for to in along_x:
+                send(q, x, others[i], to)
 
     def ring_in(q, i):
-        of = along_x[i]
-        arrived(q, of, whole)
-        for to in along_z:
-            send(q, of, to, by_ring)
-        send(q, of, sib, whole)
+        arrived(q, others_x[i], z)
+        send(q, others_x[i], z, along_z[0])
+
+    def near_in(q):
+        for i in range(1, len(others)):
+            line_in(q, i)
+            ring_in(q, i - 1)
+        for i in range(len(others) - 1, 3):
+            ring_in(q, i)
+        line_in(q, 0)
+        whole(q, x, core, 0).start()
 
     def far_in(q, i):
-        of = node(*far[i], core)
-        arrived(q, of, by_line)
-        arrived(q, of, by_ring)
-        send(q, of, sib, whole)
-
-    def turn(q, some):
-        for i in some:
-            arrived(q, chips[i] * CORES + 1 - core, whole)
-            both_cores = g[q, pl.ds(chips[i] * CORES, CORES)].reshape(both, HALF)
-            lhs[q, :, pl.ds(i * both, both)] = both_cores.T
+        for b in others:
+            arrived(q, columns[i], b)
+        whole(q, columns[i], core, i).start()
+
+    def turn(q, i):
+        whole(q, columns[i], 1 - core, i).wait_recv()
+        for b in range(line):
+            pair = g[q, :, columns[i], b].reshape(both, HALF)
+            lhs[q, :, pl.ds((i * line + b) * both, both)] = pair.T
 
     def rows(q):
         return pl.ds(HALF * (1 - q), HALF)
@@ -209,30 +226,39 @@
     def tile(j):
         return pl.ds(j * COLS, COLS)
 
-    group = len(chips) // 2
-    span = group * both
-
-    def add_group(out, patterns, q, k):
-        some = pl.ds(k * span, span)
+    span = line * both
+
+    def add_columns(out, patterns, q, first, count):
+        some = pl.ds(first * span, count * span)
         value = dot(lhs[q, :, some], patterns[some, :])
-        out[rows(q), :] = value if k == 0 else out[rows(q), :] + value
+        out[rows(q), :] = value if first == 0 else out[rows(q), :] + value
 
     def grow(q):
         for j in range(tiles):
             cols = tile(j)
             growth = p[:, cols] * jnp.exp(0.5 * heat[rows(q), cols])
-            within = split_dot(tri[...], growth)
-            depth[rows(q), cols] = within
-            tot[q, :, cols] = within[HALF - 1 :, :]
+            depth[rows(q), cols] = growth
+            tot[q, :, cols] = jnp.sum(growth, axis=0, keepdims=True)
+
+    def run_up(out, q):
+        for j in range(tiles):
+            cols = tile(j)
+            out[rows(q), cols] = split_dot(tri[...], out[rows(q), cols])
 
     @pl.when(tm + 1 < tms)
     def _():
         halo_copy().start()
 
+    for d in range(1, tms):
+
+        @pl.when(tm >= d)
+        def _():
+            pl.semaphore_signal(ready, inc=1, device_id=(tm - d, me), device_id_type=MESH)
+
+    local = lax.fori_loop(groups // 2, groups, lags(ys, HALF), local).T
+    part = local[:modes]
+    g[0, core, x, z] = local[modes:].astype(BF16)
     own(0)
-    line_in(0, 0)
-    ring_in(0, 0)
-    ring_in(0, 1)
 
     @pl.when(tm > 0)
     def _():
@@ -250,48 +276,44 @@
         yh[s] = y if s == 0 else pltpu.roll(y, s, 0)
     first = lax.fori_loop(0, 8, lags(yh, 64), jnp.zeros((64, both), F32))
     first = jnp.concatenate([first, jnp.zeros((both - 64, both), F32)], axis=0)
-    late = lax.fori_loop(8, HALF // 8, lags(yh, both), first).T
+    late = lax.fori_loop(8, groups, lags(yh, both), first).T
     late = jnp.concatenate([late[:modes], late[modes:]], axis=1)
-    g[1, me] = (part[...] + late).astype(BF16)
+    g[1, core, x, z] = (part + late).astype(BF16)
 
     own(1)
-    for i in range(1, len(others)):
-        line_in(0, i)
-    ring_in(0, 2)
-    n_near, n_far = len(near), len(far)
-    soon = 2 * n_far // 3
-    turn(0, range(n_near))
-    line_in(1, 0)
-    ring_in(1, 0)
-    ring_in(1, 1)
-    for i in range(n_far // 2):
-        far_in(0, i)
-    turn(0, range(n_near, group))
+    near_in(0)
+    turn(0, 0)
     for copy in loads[5:]:
         copy.wait()
     for i in range(len(chips)):
         for copy in pattern_loads(i):
             copy.wait()
-    add_group(heat, hh, 0, 0)
-    for i in range(1, len(others)):
-        line_in(1, i)
-    ring_in(1, 2)
-    for i in range(n_far // 2, n_far):
-        far_in(0, i)
-    add_group(load, hl, 0, 0)
-    turn(0, range(max(n_near, group), n_near + n_far))
-    add_group(heat, hh, 0, 1)
-    for i in range(soon):
-        far_in(1, i)
-    turn(1, range(group))
-    add_group(load, hl, 0, 1)
+    add_columns(heat, hh, 0, 0, 1)
+    add_columns(load, hl, 0, 0, 1)
+    near_in(1)
+    far_in(0, 1)
+    far_in(0, 2)
+    turn(1, 0)
+    add_columns(heat, hh, 1, 0, 1)
+    add_columns(load, hl, 1, 0, 1)
+    far_in(0, 3)
+    turn(0, 1)
+    turn(0, 2)
+    add_columns(heat, hh, 0, 1, 2)
+    add_columns(load, hl, 0, 1, 2)
+    far_in(1, 1)
+    far_in(1, 2)
+    turn(0, 3)
+    add_columns(heat, hh, 0, 3, 1)
     grow(0)
-    add_group(heat, hh, 1, 0)
-    for i in range(soon, n_far):
-        far_in(1, i)
-    add_group(load, hl, 1, 0)
-    turn(1, range(group, n_near + n_far))
-    add_group(heat, hh, 1, 1)
+    far_in(1, 3)
+    add_columns(load, hl, 0, 3, 1)
+    turn(1, 1)
+    turn(1, 2)
+    add_columns(heat, hh, 1, 1, 2)
+    add_columns(load, hl, 1, 1, 2)
+    turn(1, 3)
+    add_columns(heat, hh, 1, 3, 1)
     grow(1)
 
     def over(count, one):
@@ -330,8 +352,15 @@
 
         return lax.fori_loop(0, tm, one, jnp.zeros((1, points), F32))
 
+
+    @pl.when(tm + 1 < tms)
+    def _():
+        pl.semaphore_wait(ready, tms - 1 - tm)
+
     give(0)
-    add_group(load, hl, 1, 1)
+    add_columns(load, hl, 1, 3, 1)
+    run_up(depth, 1)
+    run_up(depth, 0)
     share = 8.0 / (2 * HALF * tms)
     earlier = take(0)
     rec[0, tm] = s0[...] * s0[...] + share * earlier
@@ -345,13 +374,15 @@
         layer = square * lax.rsqrt(square)
         depth[rows(q), cols] = layer
         stress = load[rows(q), cols] * (5.0 - 40.0 / (layer + 10.0))
-        within = split_dot(tri[...], stress * stress)
-        harm[rows(q), cols] = within
-        tot[2 + q, :, cols] = within[HALF - 1 :, :]
+        increment = stress * stress
+        harm[rows(q), cols] = increment
+        tot[2 + q, :, cols] = jnp.sum(increment, axis=0, keepdims=True)
 
     over(tiles, functools.partial(depth_tile, 1))
     over(tiles, functools.partial(depth_tile, 0))
     give(1)
+    run_up(harm, 1)
+    run_up(harm, 0)
     rec[1, tm] = take(1)
 
     def harm_tile(q, j):
@@ -376,8 +407,10 @@
                 total_copy(stage, d).wait_send()
 
     for q in range(2):
-        for i, part_sent in enumerate(sent[q]):
-            block(q, me, sib, i, part_sent).wait_send()
+        for i in range(sent[q]):
+            block(q, x, z, sib, i).wait_send()
+        for i in range(RING):
+            whole(q, x, core, i).wait_send()
 
 
 def writer(*refs):
@@ -405,7 +438,7 @@
     hbm = pl.BlockSpec(memory_space=pltpu.HBM)
     vmem = pl.BlockSpec(memory_space=pltpu.VMEM)
     dma = pltpu.SemaphoreType.DMA
-    sends = (line + 3) + 4 * (line - 1) + 3 * line + 3 * (line - 1)
+    sends = (line + 2) + 3 + 3 * (line - 2)
     arrays = (x, f, r, hh, hl, s0.reshape(1, points), p.reshape(1, points))
     results = pl.pallas_call(
         functools.partial(kernel, tms, line),
@@ -424,8 +457,7 @@
             pltpu.VMEM((modes, HALF), BF16),
             pltpu.VMEM((8, steps, 2 * modes), F32),
             pltpu.VMEM((8, HALF + 64, 2 * modes), F32),
-            pltpu.VMEM((modes, HALF), F32),
-            pltpu.VMEM((2, nodes, modes, HALF), BF16),
+            pltpu.VMEM((2, CORES, RING, line, modes, HALF), BF16),
             pltpu.VMEM((2, HALF, every), BF16),
             pltpu.VMEM((HALF, HALF), BF16),
             pltpu.VMEM((4, 1, points), F32),
@@ -434,10 +466,11 @@
             dma((7 + 2 * RING * line,)),
             dma((2,)),
             dma((2, sends)),
-            dma((2, nodes)),
-            dma((2, nodes)),
+            dma((2, RING * line)),
+            dma((2, 2, RING)),
             dma((2, tms)),
             dma((2, tms)),
+            pltpu.SemaphoreType.REGULAR,
         ],
         compiler_params=pltpu.CompilerParams(
             collective_id=0, has_side_effects=True, vmem_limit_bytes=40 * 1024 * 1024

time: 43.4 us -> 38.4 us (0.88)
  the two profiles are of different devices: /device:TPU:224 before, /device:TPU:136 now
where the time goes in v2:
time: 38.4 us; the launch traced here: 38.2 us
  Pallas kernels  37.6 us (98%)
  between operations  0.64 us (2%)
    pallas_call x1, Pallas kernels, shards(): pl.pallas_call(functools.partial(kernel, tms, line), out_shape=[pltpu.VME...  34.2 us
    pallas_call x1, Pallas kernels, shards(): pl.pallas_call(writer, out_shape=[jax.ShapeDtypeStruct((steps, points), F...  3.37 us

profile of v2, /device:TPU:136, one launch (start us, length us, event | category | flops | bytes accessed | tf_op | source)
XLA Modules:
  0.0 38.2 jit_solution(16816473143472743207)
XLA Ops:
  0.6 34.2 %shard_map.102 = (f32[512,1024]{1,0:T(8,128)S(1)}, f32[512,1024]{1,0:T(8,128)S(1)}, f32[512,1024]{1,0:T(8,128)S(1)}, f32[512,1024]{1,0:T(8,128)S(1)}) custom-call(bf16[64,512]{1,0:T(8,128)(2,1)} %x_in.1, bf16[64,64]{1,0:T(8,128)(2,1)} %f_in.1, f32[64,256]{1,0:T(8,128)} %r_in.1, bf16[2048,1024]{1,0:T(8,128)(2,1)} %hh_in.1, bf16[2048,1024]{1,0:T(8,128)(2,1)} %hl_in.1, ...), custom_call_target="tpu_custom_call" | custom-call | tf_op jit(solution)/shard_map/pallas_call | solution.py:443
  34.8 3.4 %shard_map.103 = (f32[512,1024]{1,0:T(8,128)}, f32[512,1024]{1,0:T(8,128)}, f32[512,1024]{1,0:T(8,128)}, f32[512,1024]{1,0:T(8,128)}) custom-call(f32[512,1024]{1,0:T(8,128)S(1)} %get-tuple-element.8.refs_0_, f32[512,1024]{1,0:T(8,128)S(1)} %get-tuple-element.9.refs_1_, f32[512,1024]{1,0:T(8,128)S(1)} %get-tuple-element.10.refs_2_, ...), custom_call_target="tpu_custom_call" | custom-call | tf_op jit(solution)/shard_map/pallas_call | solution.py:479

commit v3 on v2

--- a/solution.py
+++ b/solution.py
@@ -30,7 +30,7 @@
 def kernel(
     tms, line,
     x_in, f_in, r_in, hh_in, hl_in, s0_in, p_in,
-    heat, load, depth, harm,
+    heat, load, depth, harm, base,
     x2, fv, rv, r2, hh, hl, s0, p, halo, ys, yh, g, lhs, tri, tot, mine, rec,
     in_sem, halo_sem, ssem, rsem, bsem, xs, xr, ready,
 ):
@@ -52,13 +52,39 @@
     along_x = tuple(node(o, z, core) for o in others_x)
     if line == 4:
         upper = z // 2
-        others = (1 - z + 4 * upper, 2 - upper, 3 - 3 * upper)
+        beside = 1 - z + 4 * upper
+        others = (beside, lax.rem(z + 2, line), lax.rem(beside + 2, line))
     else:
         others = (1 - z,)
     along_z = tuple(node(x, o, core) for o in others)
     columns = (x, *others_x)
     chips = [a * line + b for a in columns for b in range(line)]
     both = CORES * modes
+
+    barrier = pltpu.get_barrier_semaphore()
+
+    span = tms // 2
+    mid = line // 2
+    crossed_in = 1 - lax.min(1, lax.rem(tm, span))
+    crossed_out = 1 - lax.min(1, lax.rem(tm + 1, span))
+    at_end = 1 - lax.min(1, lax.rem(z, line - 1))
+    nearer = (line - 1) * (1 - z // mid)
+    server = node(x, z + crossed_in * (nearer - z), core)
+    served = (1 - (tm + 1) // tms) * (1 - crossed_out + crossed_out * at_end * mid)
+
+    @pl.when(tm > 0)
+    def _():
+        pl.semaphore_signal(barrier, inc=1, device_id=(tm - 1, server), device_id_type=MESH)
+
+
+    for d in range(1, tms):
+
+        @pl.when(tm + d < tms)
+        def _():
+            pl.semaphore_signal(barrier, inc=1, device_id=(tm + d, me), device_id_type=MESH)
+
+    for other in (sib, *along_x, *along_z):
+        pl.semaphore_signal(barrier, inc=1, device_id=(tm, other), device_id_type=MESH)
 
     loads = [
         pltpu.make_async_copy(a, b, in_sem.at[i])
@@ -83,21 +109,6 @@
 
     for copy in loads:
         copy.start()
-
-    barrier = pltpu.get_barrier_semaphore()
-    for other in (sib, *along_x, *along_z):
-        pl.semaphore_signal(barrier, inc=1, device_id=(tm, other), device_id_type=MESH)
-    for d in range(1, tms):
-
-        @pl.when(tm + d < tms)
-        def _():
-            pl.semaphore_signal(barrier, inc=1, device_id=(tm + d, me), device_id_type=MESH)
-
-    @pl.when(tm > 0)
-    def _():
-        pl.semaphore_signal(barrier, inc=1, device_id=(tm - 1, me), device_id_type=MESH)
-
-
     for i in range(len(chips)):
         for copy in pattern_loads(i):
             copy.start()
@@ -141,17 +152,19 @@
         return some
 
     groups = HALF // 8
-    local = lax.fori_loop(0, groups // 2, lags(ys, HALF), jnp.zeros((HALF, both), F32))
-
-    pl.semaphore_wait(barrier, 4 + len(others) + tm + 1 - (tm + 1) // tms)
-
-    def halo_copy():
+    turns = groups // 2 + groups // 2 * lax.min(1, tm // span)
+    local = lax.fori_loop(0, turns, lags(ys, HALF), jnp.zeros((HALF, both), F32))
+
+    pl.semaphore_wait(barrier, 4 + len(others) + tm + served)
+
+    def halo_copy(i):
+        there = z + crossed_out * (i + mid * (1 - lax.min(1, z)) - z)
         return pltpu.make_async_remote_copy(
             src_ref=x2.at[pl.ds(modes, modes), pl.ds(HALF, HALF)],
             dst_ref=halo,
-            send_sem=halo_sem.at[0],
-            recv_sem=halo_sem.at[1],
-            device_id=(lax.rem(tm + 1, tms), me),
+            send_sem=halo_sem.at[i],
+            recv_sem=halo_sem.at[mid],
+            device_id=(lax.rem(tm + 1, tms), node(x, there, core)),
             device_id_type=MESH,
         )
 
@@ -187,27 +200,28 @@
         sent[q] += 1
 
     def own(q):
-        for to in (*along_z[1:], *along_x[:2], along_z[0], along_x[2]):
+        for to in (*along_z[1:], *along_x[::-1], along_z[0]):
             send(q, x, z, to)
 
     def line_in(q, i):
         arrived(q, x, others[i])
         if i > 0:
-            for to in along_x:
+            for to in along_x[::-1]:
                 send(q, x, others[i], to)
 
     def ring_in(q, i):
         arrived(q, others_x[i], z)
         send(q, others_x[i], z, along_z[0])
 
-    def near_in(q):
-        for i in range(1, len(others)):
-            line_in(q, i)
-            ring_in(q, i - 1)
-        for i in range(len(others) - 1, 3):
-            ring_in(q, i)
-        line_in(q, 0)
-        whole(q, x, core, 0).start()
+    def near_in():
+        for q in range(2):
+            for i in range(1, len(others)):
+                line_in(q, i)
+            for i in range(3):
+                ring_in(q, i)
+        for q in range(2):
+            line_in(q, 0)
+            whole(q, x, core, 0).start()
 
     def far_in(q, i):
         for b in others:
@@ -245,9 +259,11 @@
             cols = tile(j)
             out[rows(q), cols] = split_dot(tri[...], out[rows(q), cols])
 
-    @pl.when(tm + 1 < tms)
-    def _():
-        halo_copy().start()
+    for i in range(mid):
+
+        @pl.when(served > i)
+        def _():
+            halo_copy(i).start()
 
     for d in range(1, tms):
 
@@ -255,14 +271,14 @@
         def _():
             pl.semaphore_signal(ready, inc=1, device_id=(tm - d, me), device_id_type=MESH)
 
-    local = lax.fori_loop(groups // 2, groups, lags(ys, HALF), local).T
+    local = lax.fori_loop(turns, groups, lags(ys, HALF), local).T
     part = local[:modes]
     g[0, core, x, z] = local[modes:].astype(BF16)
     own(0)
 
     @pl.when(tm > 0)
     def _():
-        halo_copy().wait_recv()
+        halo_copy(0).wait_recv()
 
     @pl.when(tm == 0)
     def _():
@@ -281,39 +297,31 @@
     g[1, core, x, z] = (part + late).astype(BF16)
 
     own(1)
-    near_in(0)
+    near_in()
     turn(0, 0)
     for copy in loads[5:]:
         copy.wait()
     for i in range(len(chips)):
         for copy in pattern_loads(i):
             copy.wait()
+    rest = RING - 1
     add_columns(heat, hh, 0, 0, 1)
     add_columns(load, hl, 0, 0, 1)
-    near_in(1)
-    far_in(0, 1)
-    far_in(0, 2)
     turn(1, 0)
     add_columns(heat, hh, 1, 0, 1)
+    for i in range(1, RING):
+        far_in(0, i)
     add_columns(load, hl, 1, 0, 1)
-    far_in(0, 3)
-    turn(0, 1)
-    turn(0, 2)
-    add_columns(heat, hh, 0, 1, 2)
-    add_columns(load, hl, 0, 1, 2)
-    far_in(1, 1)
-    far_in(1, 2)
-    turn(0, 3)
-    add_columns(heat, hh, 0, 3, 1)
+    for i in range(1, RING):
+        turn(0, i)
+    add_columns(heat, hh, 0, 1, rest)
     grow(0)
-    far_in(1, 3)
-    add_columns(load, hl, 0, 3, 1)
-    turn(1, 1)
-    turn(1, 2)
-    add_columns(heat, hh, 1, 1, 2)
-    add_columns(load, hl, 1, 1, 2)
-    turn(1, 3)
-    add_columns(heat, hh, 1, 3, 1)
+    for i in range(1, RING):
+        far_in(1, i)
+    add_columns(load, hl, 0, 1, rest)
+    for i in range(1, RING):
+        turn(1, i)
+    add_columns(heat, hh, 1, 1, rest)
     grow(1)
 
     def over(count, one):
@@ -358,19 +366,32 @@
         pl.semaphore_wait(ready, tms - 1 - tm)
 
     give(0)
-    add_columns(load, hl, 1, 3, 1)
+    add_columns(load, hl, 1, 1, rest)
     run_up(depth, 1)
     run_up(depth, 0)
+
+    for i in range(mid):
+
+        @pl.when(served > i)
+        def _():
+            halo_copy(i).wait_send()
+
+    for q in range(2):
+        for i in range(sent[q]):
+            block(q, x, z, sib, i).wait_send()
+        for i in range(RING):
+            whole(q, x, core, i).wait_send()
+
     share = 8.0 / (2 * HALF * tms)
     earlier = take(0)
     rec[0, tm] = s0[...] * s0[...] + share * earlier
 
     def depth_tile(q, j):
         cols = tile(j)
-        base = rec[0, tm, :, cols]
+        start = rec[0, tm, :, cols]
         if q == 0:
-            base = base + share * tot[1, :, cols]
-        square = base + share * depth[rows(q), cols]
+            start = start + share * tot[1, :, cols]
+        square = start + share * depth[rows(q), cols]
         layer = square * lax.rsqrt(square)
         depth[rows(q), cols] = layer
         stress = load[rows(q), cols] * (5.0 - 40.0 / (layer + 10.0))
@@ -385,19 +406,8 @@
     run_up(harm, 0)
     rec[1, tm] = take(1)
 
-    def harm_tile(q, j):
-        cols = tile(j)
-        base = rec[1, tm, :, cols]
-        if q == 0:
-            base = base + tot[3, :, cols]
-        harm[rows(q), cols] = (harm[rows(q), cols] + base) * (1.0 / (2 * HALF * tms))
-
-    over(tiles, functools.partial(harm_tile, 1))
-    over(tiles, functools.partial(harm_tile, 0))
-
-    @pl.when(tm + 1 < tms)
-    def _():
-        halo_copy().wait_send()
+    base[0] = rec[1, tm]
+    base[1] = rec[1, tm] + tot[3]
 
     for stage in range(2):
         for d in range(1, tms):
@@ -406,27 +416,26 @@
             def _():
                 total_copy(stage, d).wait_send()
 
-    for q in range(2):
-        for i in range(sent[q]):
-            block(q, x, z, sib, i).wait_send()
-        for i in range(RING):
-            whole(q, x, core, i).wait_send()
-
-
-def writer(*refs):
-    sem = refs[8]
-    size = refs[0].shape[0] // PIECES
-    copies = [
-        pltpu.make_async_copy(
-            refs[i].at[pl.ds(k * size, size)], refs[4 + i].at[pl.ds(k * size, size)], sem.at[i, k]
-        )
-        for i in range(4)
-        for k in range(PIECES)
-    ]
-    for copy in copies:
-        copy.start()
-    for copy in copies:
-        copy.wait()
+
+def writer(steps, heat, load, depth, harm, base, *refs):
+    outs, total, sem = refs[:4], refs[4], refs[5]
+    ins = (heat, load, depth, total)
+    size = HALF
+
+    def copy(i, k):
+        part = pl.ds(k * size, size)
+        return pltpu.make_async_copy(ins[i].at[part], outs[i].at[part], sem.at[i, k])
+
+    for i in range(3):
+        for k in range(PIECES):
+            copy(i, k).start()
+    for k in range(PIECES):
+        part = pl.ds(k * size, size)
+        total[part] = (harm[part] + base[k]) * (1.0 / steps)
+        copy(3, k).start()
+    for i in range(4):
+        for k in range(PIECES):
+            copy(i, k).wait()
 
 
 def shards(tms, line, x, f, r, hh, hl, s0, p):
@@ -442,9 +451,9 @@
     arrays = (x, f, r, hh, hl, s0.reshape(1, points), p.reshape(1, points))
     results = pl.pallas_call(
         functools.partial(kernel, tms, line),
-        out_shape=[pltpu.VMEM((steps, points), F32)] * 4,
+        out_shape=[pltpu.VMEM((steps, points), F32)] * 4 + [pltpu.VMEM((2, 1, points), F32)],
         in_specs=[hbm] * 7,
-        out_specs=[vmem] * 4,
+        out_specs=[vmem] * 5,
         scratch_shapes=[
             pltpu.VMEM((2 * modes, steps), BF16),
             pltpu.VMEM(f.shape, BF16),
@@ -464,7 +473,7 @@
             pltpu.VMEM((2, 1, points), F32),
             pltpu.VMEM((2, tms, 1, points), F32),
             dma((7 + 2 * RING * line,)),
-            dma((2,)),
+            dma((line // 2 + 1,)),
             dma((2, sends)),
             dma((2, RING * line)),
             dma((2, 2, RING)),
@@ -477,12 +486,12 @@
         ),
     )(*(pltpu.with_memory_space_constraint(a, pltpu.HBM) for a in arrays))
     return pl.pallas_call(
-        writer,
+        functools.partial(writer, steps * tms),
         out_shape=[jax.ShapeDtypeStruct((steps, points), F32)] * 4,
-        in_specs=[vmem] * 4,
+        in_specs=[vmem] * 5,
         out_specs=[pl.BlockSpec(memory_space=pl.ANY)] * 4,
-        scratch_shapes=[dma((4, PIECES))],
-        compiler_params=pltpu.CompilerParams(vmem_limit_bytes=4 * 1024 * 1024),
+        scratch_shapes=[pltpu.VMEM((steps, points), F32), dma((4, PIECES))],
+        compiler_params=pltpu.CompilerParams(vmem_limit_bytes=6 * 1024 * 1024),
     )(*results)
 
 

time: 38.4 us -> 36 us (0.938)
  the two profiles are of different devices: /device:TPU:136 before, /device:TPU:224 now
where the time goes in v3:
time: 36 us; the launch traced here: 35.8 us
  Pallas kernels  35.2 us (98%)
  between operations  0.64 us (2%)
    pallas_call x1, Pallas kernels, shards(): pl.pallas_call(functools.partial(kernel, tms, line), out_shape=[pltpu.VME...  31.8 us
    pallas_call x1, Pallas kernels, shards(): pl.pallas_call(functools.partial(writer, steps * tms), out_shape=[jax.Sha...  3.37 us

profile of v3, /device:TPU:224, one launch (start us, length us, event | category | flops | bytes accessed | tf_op | source)
XLA Modules:
  0.0 35.8 jit_solution(4828487401386705501)
XLA Ops:
  0.6 31.8 %shard_map.102 = (f32[512,1024]{1,0:T(8,128)S(1)}, f32[512,1024]{1,0:T(8,128)S(1)}, f32[512,1024]{1,0:T(8,128)S(1)}, f32[512,1024]{1,0:T(8,128)S(1)}, f32[2,1,1024]{2,1,0:T(1,128)S(1)}) custom-call(bf16[64,512]{1,0:T(8,128)(2,1)} %x_in.1, bf16[64,64]{1,0:T(8,128)(2,1)} %f_in.1, f32[64,256]{1,0:T(8,128)} %r_in.1, bf16[2048,1024]{1,0:T(8,128)(2,1)} %hh_in.1, ...), custom_call_target="tpu_custom_call" | custom-call | tf_op jit(solution)/shard_map/pallas_call | solution.py:452
  32.5 3.4 %shard_map.103 = (f32[512,1024]{1,0:T(8,128)}, f32[512,1024]{1,0:T(8,128)}, f32[512,1024]{1,0:T(8,128)}, f32[512,1024]{1,0:T(8,128)}) custom-call(f32[512,1024]{1,0:T(8,128)S(1)} %get-tuple-element.9.heat, f32[512,1024]{1,0:T(8,128)S(1)} %get-tuple-element.10.load, f32[512,1024]{1,0:T(8,128)S(1)} %get-tuple-element.11.depth, ...), custom_call_target="tpu_custom_call" | custom-call | tf_op jit(solution)/shard_map/pallas_call | solution.py:488

commit v4 on v3

--- a/solution.py
+++ b/solution.py
@@ -141,19 +141,22 @@
     for s in range(8):
         ys[s] = y if s == 0 else pltpu.roll(y, s, 0)
 
-    def lags(source, rows):
+    def lags(source, rows, down=0):
         def some(a, total):
             at = pl.multiple_of(HALF - 8 * a, 8)
             weights = r2[pl.ds(pl.multiple_of(8 * a, 8), 8), :]
             for s in range(8):
-                total = total + weights[s : s + 1, :] * source[s, pl.ds(at, rows), :]
+                total = total + weights[s : s + 1, :] * source[s, pl.ds(at + down, rows), :]
             return total
 
         return some
 
     groups = HALF // 8
     turns = groups // 2 + groups // 2 * lax.min(1, tm // span)
-    local = lax.fori_loop(0, turns, lags(ys, HALF), jnp.zeros((HALF, both), F32))
+    blocks = range(0, HALF, both)
+    local = [
+        lax.fori_loop(0, turns, lags(ys, both, i), jnp.zeros((both, both), F32)) for i in blocks
+    ]
 
     pl.semaphore_wait(barrier, 4 + len(others) + tm + served)
 
@@ -240,15 +243,21 @@
     def tile(j):
         return pl.ds(j * COLS, COLS)
 
-    span = line * both
-
-    def add_columns(out, patterns, q, first, count):
-        some = pl.ds(first * span, count * span)
-        value = dot(lhs[q, :, some], patterns[some, :])
-        out[rows(q), :] = value if first == 0 else out[rows(q), :] + value
-
-    def grow(q):
-        for j in range(tiles):
+    width = line * both
+
+    def add_columns(out, patterns, q, first, count, nodes=pl.ds(0, points)):
+        some = pl.ds(first * width, count * width)
+        value = dot(lhs[q, :, some], patterns[some, nodes])
+        out[rows(q), nodes] = value if first == 0 else out[rows(q), nodes] + value
+
+    per = tiles // 2
+    ranges = [pl.ds(h * per * COLS, per * COLS) for h in range(2)]
+
+    def in_range(h):
+        return range(h * per, (h + 1) * per)
+
+    def grow(q, h):
+        for j in in_range(h):
             cols = tile(j)
             growth = p[:, cols] * jnp.exp(0.5 * heat[rows(q), cols])
             depth[rows(q), cols] = growth
@@ -259,6 +268,17 @@
             cols = tile(j)
             out[rows(q), cols] = split_dot(tri[...], out[rows(q), cols])
 
+    share = 8.0 / (2 * HALF * tms)
+
+    def settle(q):
+        run_up(depth, q)
+        for j in range(tiles):
+            cols = tile(j)
+            start = s0[:, cols] * s0[:, cols]
+            if q == 0:
+                start = start + share * tot[1, :, cols]
+            depth[rows(q), cols] = start + share * depth[rows(q), cols]
+
     for i in range(mid):
 
         @pl.when(served > i)
@@ -271,7 +291,10 @@
         def _():
             pl.semaphore_signal(ready, inc=1, device_id=(tm - d, me), device_id_type=MESH)
 
-    local = lax.fori_loop(turns, groups, lags(ys, HALF), local).T
+    local = [
+        lax.fori_loop(turns, groups, lags(ys, both, i), some) for i, some in zip(blocks, local)
+    ]
+    local = jnp.concatenate(local, axis=0).T
     part = local[:modes]
     g[0, core, x, z] = local[modes:].astype(BF16)
     own(0)
@@ -315,60 +338,61 @@
     for i in range(1, RING):
         turn(0, i)
     add_columns(heat, hh, 0, 1, rest)
-    grow(0)
+    grow(0, 0)
+    grow(0, 1)
     for i in range(1, RING):
         far_in(1, i)
     add_columns(load, hl, 0, 1, rest)
     for i in range(1, RING):
         turn(1, i)
-    add_columns(heat, hh, 1, 1, rest)
-    grow(1)
-
-    def over(count, one):
-        for j in range(count):
-            one(j)
-
-    def total_copy(stage, d):
+
+    def total_copy(stage, h, d):
         return pltpu.make_async_remote_copy(
-            src_ref=mine.at[stage],
-            dst_ref=rec.at[stage, tm],
-            send_sem=xs.at[stage, d],
-            recv_sem=xr.at[stage, tm],
+            src_ref=mine.at[stage, :, ranges[h]],
+            dst_ref=rec.at[stage, tm, :, ranges[h]],
+            send_sem=xs.at[stage, h, d],
+            recv_sem=xr.at[stage, h, tm],
             device_id=(lax.rem(tm + d, tms), me),
             device_id_type=MESH,
         )
 
-    def give(stage):
-        mine[stage] = tot[2 * stage] + tot[2 * stage + 1]
+    def give(stage, h):
+        nodes = ranges[h]
+        mine[stage, :, nodes] = tot[2 * stage, :, nodes] + tot[2 * stage + 1, :, nodes]
         for d in range(tms - 1, 0, -1):
 
             @pl.when(tm + d < tms)
             def _():
-                total_copy(stage, d).start()
-
-    def take(stage):
+                total_copy(stage, h, d).start()
+
+    def take(stage, h):
         def one(i, total):
             pltpu.make_async_remote_copy(
-                src_ref=mine.at[stage],
-                dst_ref=rec.at[stage, i],
-                send_sem=xs.at[stage, 0],
-                recv_sem=xr.at[stage, i],
+                src_ref=mine.at[stage, :, ranges[h]],
+                dst_ref=rec.at[stage, i, :, ranges[h]],
+                send_sem=xs.at[stage, h, 0],
+                recv_sem=xr.at[stage, h, i],
                 device_id=(lax.rem(tm + 1, tms), me),
                 device_id_type=MESH,
             ).wait_recv()
-            return total + rec[stage, i]
-
-        return lax.fori_loop(0, tm, one, jnp.zeros((1, points), F32))
-
+            return total + rec[stage, i, :, ranges[h]]
+
+        return lax.fori_loop(0, tm, one, jnp.zeros((1, per * COLS), F32))
+
+    add_columns(heat, hh, 1, 1, rest, ranges[0])
+    grow(1, 0)
 
     @pl.when(tm + 1 < tms)
     def _():
         pl.semaphore_wait(ready, tms - 1 - tm)
 
-    give(0)
+    give(0, 0)
+    add_columns(heat, hh, 1, 1, rest, ranges[1])
+    grow(1, 1)
+    give(0, 1)
     add_columns(load, hl, 1, 1, rest)
-    run_up(depth, 1)
-    run_up(depth, 0)
+    settle(1)
+    settle(0)
 
     for i in range(mid):
 
@@ -383,15 +407,10 @@
             whole(q, x, core, i).wait_send()
 
     share = 8.0 / (2 * HALF * tms)
-    earlier = take(0)
-    rec[0, tm] = s0[...] * s0[...] + share * earlier
 
     def depth_tile(q, j):
         cols = tile(j)
-        start = rec[0, tm, :, cols]
-        if q == 0:
-            start = start + share * tot[1, :, cols]
-        square = start + share * depth[rows(q), cols]
+        square = rec[0, tm, :, cols] + depth[rows(q), cols]
         layer = square * lax.rsqrt(square)
         depth[rows(q), cols] = layer
         stress = load[rows(q), cols] * (5.0 - 40.0 / (layer + 10.0))
@@ -399,22 +418,26 @@
         harm[rows(q), cols] = increment
         tot[2 + q, :, cols] = jnp.sum(increment, axis=0, keepdims=True)
 
-    over(tiles, functools.partial(depth_tile, 1))
-    over(tiles, functools.partial(depth_tile, 0))
-    give(1)
+    for h in range(2):
+        rec[0, tm, :, ranges[h]] = share * take(0, h)
+        for j in in_range(h):
+            depth_tile(1, j)
+            depth_tile(0, j)
+        give(1, h)
     run_up(harm, 1)
     run_up(harm, 0)
-    rec[1, tm] = take(1)
-
-    base[0] = rec[1, tm]
-    base[1] = rec[1, tm] + tot[3]
+    for h in range(2):
+        earlier = take(1, h)
+        base[0, :, ranges[h]] = earlier
+        base[1, :, ranges[h]] = earlier + tot[3, :, ranges[h]]
 
     for stage in range(2):
-        for d in range(1, tms):
-
-            @pl.when(tm + d < tms)
-            def _():
-                total_copy(stage, d).wait_send()
+        for h in range(2):
+            for d in range(1, tms):
+
+                @pl.when(tm + d < tms)
+                def _():
+                    total_copy(stage, h, d).wait_send()
 
 
 def writer(steps, heat, load, depth, harm, base, *refs):
@@ -477,8 +500,8 @@
             dma((2, sends)),
             dma((2, RING * line)),
             dma((2, 2, RING)),
-            dma((2, tms)),
-            dma((2, tms)),
+            dma((2, 2, tms)),
+            dma((2, 2, tms)),
             pltpu.SemaphoreType.REGULAR,
         ],
         compiler_params=pltpu.CompilerParams(

time: 36 us -> 34.9 us (0.969)
  Pallas kernels: 35.2 us -> 34.1 us
    pallas_call x1, Pallas kernels: 31.8 us -> 30.7 us  [shards(): pl.pallas_call(functools.partial(kernel, tms, line), out_shape=[pltpu.VME...]
where the time goes in v4:
time: 34.9 us; the launch traced here: 34.7 us
  Pallas kernels  34.1 us (98%)
  between operations  0.64 us (2%)
    pallas_call x1, Pallas kernels, shards(): pl.pallas_call(functools.partial(kernel, tms, line), out_shape=[pltpu.VME...  30.7 us
    pallas_call x1, Pallas kernels, shards(): pl.pallas_call(functools.partial(writer, steps * tms), out_shape=[jax.Sha...  3.37 us

profile of v4, /device:TPU:224, one launch (start us, length us, event | category | flops | bytes accessed | tf_op | source)
XLA Modules:
  0.0 34.7 jit_solution(6718400245092488835)
XLA Ops:
  0.6 30.7 %shard_map.102 = (f32[512,1024]{1,0:T(8,128)S(1)}, f32[512,1024]{1,0:T(8,128)S(1)}, f32[512,1024]{1,0:T(8,128)S(1)}, f32[512,1024]{1,0:T(8,128)S(1)}, f32[2,1,1024]{2,1,0:T(1,128)S(1)}) custom-call(bf16[64,512]{1,0:T(8,128)(2,1)} %x_in.1, bf16[64,64]{1,0:T(8,128)(2,1)} %f_in.1, f32[64,256]{1,0:T(8,128)} %r_in.1, bf16[2048,1024]{1,0:T(8,128)(2,1)} %hh_in.1, ...), custom_call_target="tpu_custom_call" | custom-call | tf_op jit(solution)/shard_map/pallas_call | solution.py:475
  31.4 3.4 %shard_map.103 = (f32[512,1024]{1,0:T(8,128)}, f32[512,1024]{1,0:T(8,128)}, f32[512,1024]{1,0:T(8,128)}, f32[512,1024]{1,0:T(8,128)}) custom-call(f32[512,1024]{1,0:T(8,128)S(1)} %get-tuple-element.9.heat, f32[512,1024]{1,0:T(8,128)S(1)} %get-tuple-element.10.load, f32[512,1024]{1,0:T(8,128)S(1)} %get-tuple-element.11.depth, ...), custom_call_target="tpu_custom_call" | custom-call | tf_op jit(solution)/shard_map/pallas_call | solution.py:511

commit v5 on v4

--- a/solution.py
+++ b/solution.py
@@ -120,16 +120,11 @@
     for copy in loads[:5]:
         copy.wait()
 
-    twice = (
-        lax.rem(lax.broadcasted_iota(jnp.int32, (both, modes), 0), modes)
-        == lax.broadcasted_iota(jnp.int32, (both, modes), 1)
-    ).astype(F32).astype(BF16)
-    wide = lax.dot_general(dot(twice, fv[...]).astype(BF16), twice, NT, preferred_element_type=F32)
-    same = (
-        lax.broadcasted_iota(jnp.int32, (both, both), 0) // modes
-        == lax.broadcasted_iota(jnp.int32, (both, both), 1) // modes
-    )
-    drive = jnp.where(same, wide, 0.0).astype(BF16)
+    force = fv[...].astype(F32)
+    none = jnp.zeros_like(force)
+    drive = jnp.concatenate(
+        [jnp.concatenate([force, none], axis=1), jnp.concatenate([none, force], axis=1)], axis=0
+    ).astype(BF16)
 
     def driven(source):
         return lax.dot_general(

time: 34.9 us -> 34.9 us (level)
  no operation moved by 1% of the time
where the time goes in v5:
time: 34.9 us; the launch traced here: 34.7 us
  Pallas kernels  34 us (97%)
  between operations  0.64 us (2%)
    pallas_call x1, Pallas kernels, shards(): pl.pallas_call(functools.partial(kernel, tms, line), out_shape=[pltpu.VME...  30.7 us
    pallas_call x1, Pallas kernels, shards(): pl.pallas_call(functools.partial(writer, steps * tms), out_shape=[jax.Sha...  3.37 us

profile of v5, /device:TPU:224, one launch (start us, length us, event | category | flops | bytes accessed | tf_op | source)
XLA Modules:
  0.0 34.7 jit_solution(79723351772506504)
XLA Ops:
  0.6 30.7 %shard_map.102 = (f32[512,1024]{1,0:T(8,128)S(1)}, f32[512,1024]{1,0:T(8,128)S(1)}, f32[512,1024]{1,0:T(8,128)S(1)}, f32[512,1024]{1,0:T(8,128)S(1)}, f32[2,1,1024]{2,1,0:T(1,128)S(1)}) custom-call(bf16[64,512]{1,0:T(8,128)(2,1)} %x_in.1, bf16[64,64]{1,0:T(8,128)(2,1)} %f_in.1, f32[64,256]{1,0:T(8,128)} %r_in.1, bf16[2048,1024]{1,0:T(8,128)(2,1)} %hh_in.1, ...), custom_call_target="tpu_custom_call" | custom-call | tf_op jit(solution)/shard_map/pallas_call | solution.py:470
  31.3 3.4 %shard_map.103 = (f32[512,1024]{1,0:T(8,128)}, f32[512,1024]{1,0:T(8,128)}, f32[512,1024]{1,0:T(8,128)}, f32[512,1024]{1,0:T(8,128)}) custom-call(f32[512,1024]{1,0:T(8,128)S(1)} %get-tuple-element.9.heat, f32[512,1024]{1,0:T(8,128)S(1)} %get-tuple-element.10.load, f32[512,1024]{1,0:T(8,128)S(1)} %get-tuple-element.11.depth, ...), custom_call_target="tpu_custom_call" | custom-call | tf_op jit(solution)/shard_map/pallas_call | solution.py:506

commit v6 on v5

--- a/solution.py
+++ b/solution.py
@@ -117,8 +117,7 @@
         lax.broadcasted_iota(jnp.int32, (HALF, HALF), 0)
         >= lax.broadcasted_iota(jnp.int32, (HALF, HALF), 1)
     ).astype(F32).astype(BF16)
-    for copy in loads[:5]:
-        copy.wait()
+    loads[0].wait()
 
     force = fv[...].astype(F32)
     none = jnp.zeros_like(force)
@@ -131,10 +130,14 @@
             source.astype(F32).T.astype(BF16), drive, NT, preferred_element_type=F32
         )
 
-    r2[...] = rv[...].T
+    for copy in loads[1:3]:
+        copy.wait()
     y = driven(x2[...])
     for s in range(8):
         ys[s] = y if s == 0 else pltpu.roll(y, s, 0)
+    for copy in loads[3:5]:
+        copy.wait()
+    r2[...] = rv[...].T
 
     def lags(source, rows, down=0):
         def some(a, total):

time: 34.9 us -> 34.9 us (level)
  no operation moved by 1% of the time
where the time goes in v6:
time: 34.9 us; the launch traced here: 34.7 us
  Pallas kernels  34 us (97%)
  between operations  0.64 us (2%)
    pallas_call x1, Pallas kernels, shards(): pl.pallas_call(functools.partial(kernel, tms, line), out_shape=[pltpu.VME...  30.7 us
    pallas_call x1, Pallas kernels, shards(): pl.pallas_call(functools.partial(writer, steps * tms), out_shape=[jax.Sha...  3.37 us

profile of v6, /device:TPU:224, one launch (start us, length us, event | category | flops | bytes accessed | tf_op | source)
XLA Modules:
  0.0 34.7 jit_solution(15679060032702092944)
XLA Ops:
  0.6 30.7 %shard_map.102 = (f32[512,1024]{1,0:T(8,128)S(1)}, f32[512,1024]{1,0:T(8,128)S(1)}, f32[512,1024]{1,0:T(8,128)S(1)}, f32[512,1024]{1,0:T(8,128)S(1)}, f32[2,1,1024]{2,1,0:T(1,128)S(1)}) custom-call(bf16[64,512]{1,0:T(8,128)(2,1)} %x_in.1, bf16[64,64]{1,0:T(8,128)(2,1)} %f_in.1, f32[64,256]{1,0:T(8,128)} %r_in.1, bf16[2048,1024]{1,0:T(8,128)(2,1)} %hh_in.1, ...), custom_call_target="tpu_custom_call" | custom-call | tf_op jit(solution)/shard_map/pallas_call | solution.py:473
  31.3 3.4 %shard_map.103 = (f32[512,1024]{1,0:T(8,128)}, f32[512,1024]{1,0:T(8,128)}, f32[512,1024]{1,0:T(8,128)}, f32[512,1024]{1,0:T(8,128)}) custom-call(f32[512,1024]{1,0:T(8,128)S(1)} %get-tuple-element.9.heat, f32[512,1024]{1,0:T(8,128)S(1)} %get-tuple-element.10.load, f32[512,1024]{1,0:T(8,128)S(1)} %get-tuple-element.11.depth, ...), custom_call_target="tpu_custom_call" | custom-call | tf_op jit(solution)/shard_map/pallas_call | solution.py:509
